TPU v7x, 256 devices: a whole 4x4x8 slice. The times are simulated.
256 devices in a mesh: chan: 16 (over x, z_hi), band: 16 (over z_lo, y, core).
Axes of the slice: x: 4, y: 4, z: 8 (z_hi: 4, z_lo: 2; z = z_hi * 2 + z_lo), core: 2. Of those that a mesh axis runs over, the one named last changes fastest.
Arguments:
- spectra: bfloat16 [32, 2, 8192, 512], P('band', None, 'chan'), may hold values from -64 to 64
- half_width: int32 [512], replicated, may hold values from 1 to 32, as said below
- panel_block: int32 [4], replicated, may hold values from 0 to 15
- panel_offset: int32 [4], replicated, may hold values from 0 to 256
Outputs:
- cross: bfloat16 [4, 32, 2, 8192, 256], P(None, 'band', None, 'chan')
Inputs may be any that keep to these rules, and one draw needn't show every extreme that they name: `half_width`: some window's half-width is exactly 32.
All inputs are finite; a program needn't handle non-finite values.
Results may differ from a plain program's by a relative error of at most 0.0056.
Values may be sent and summed in bfloat16 or wider, within the bound.
A program may use at most 64 MiB of HBM per device.

v0:
```python
import jax
import jax.numpy as jnp
from jax import lax
from jax.sharding import PartitionSpec as P

PANEL = 256
NPANEL = 4
HALO = 32


def with_halo(block, sides, width):
    for axis, dim in sides:
        count = lax.axis_size(axis)
        forward = [(i, i + 1) for i in range(count - 1)]
        backward = [(target, source) for source, target in forward]
        low = lax.ppermute(
            lax.slice_in_dim(block, block.shape[dim] - width, None, axis=dim), axis, forward
        )
        high = lax.ppermute(lax.slice_in_dim(block, 0, width, axis=dim), axis, backward)
        block = jnp.concatenate([low, block, high], axis=dim)
    return block


def from_root(block, axis, holder):
    block = jnp.where(lax.axis_index(axis) == holder, block, jnp.zeros_like(block))
    return lax.psum(block, axis)


def norm_scale(power, widths, first_chan, channels, bins):
    rows = power.shape[0]
    padded = with_halo(power, (("chan", 0),), HALO)
    total = jnp.zeros_like(power)
    for offset in range(-HALO, HALO + 1):
        window = padded[HALO + offset : HALO + offset + rows]
        total = total + jnp.where(abs(offset) <= widths[None, :], window, jnp.float32(0.0))
    chan_index = jnp.arange(rows, dtype=jnp.int32)[:, None] + first_chan
    count = (
        jnp.minimum(chan_index + widths[None, :], channels - 1)
        - jnp.maximum(chan_index - widths[None, :], 0)
        + 1
    )
    return lax.rsqrt(total / (count.astype(jnp.float32) * bins) + 1e-06)


def local(spectra, half_width, panel_block, panel_offset):
    f_dev, parts, ch_dev, windows = spectra.shape
    bins = f_dev * lax.axis_size("band")
    channels = ch_dev * lax.axis_size("chan")
    block_here = lax.axis_index("chan")
    first_chan = block_here * ch_dev
    local_power = jnp.sum(jnp.square(spectra.astype(jnp.float32)), axis=(0, 1))
    power = lax.psum(local_power, "band")
    scale = norm_scale(power, half_width, first_chan, channels, bins)
    normed = (spectra.astype(jnp.float32) * scale[None, None]).astype(jnp.bfloat16)
    flat = normed.reshape(f_dev, 2 * ch_dev, windows)
    results = []
    for panel in range(NPANEL):
        source = from_root(
            lax.dynamic_slice_in_dim(normed, panel_offset[panel], PANEL, 2),
            "chan",
            panel_block[panel],
        )
        right = source.reshape(f_dev, 2 * PANEL, windows)
        grams = jnp.einsum("fxw,fyw->fxy", flat, right, preferred_element_type=jnp.float32)
        real_part = grams[:, :ch_dev, :PANEL] + grams[:, ch_dev:, PANEL:]
        imag_part = grams[:, ch_dev:, :PANEL] - grams[:, :ch_dev, PANEL:]
        results.append(
            (jnp.stack([real_part, imag_part], axis=1) * windows ** (-0.5)).astype(jnp.bfloat16)
        )
    return jnp.stack(results)


def solution(mesh):
    placed = (P("band", None, "chan", None), P(), P(), P())
    return jax.shard_map(
        local,
        mesh=mesh,
        in_specs=placed,
        out_specs=P(None, "band", None, "chan", None),
        check_vma=False,
    )
```

profile of v0, /device:TPU:8, one launch (start us, length us, event | category | flops | bytes accessed | tf_op | source)
XLA Modules:
  0.0 410.5 jit_solution(6343302866503739388)
XLA Ops:
  6.5 3.1 fusion
  9.7 0.7 fusion.83
  15.4 0.7 fusion.82
  21.1 112.6 %all-reduce.4.cloned.1.call-done = f32[512,512]{1,0:T(8,128)} async-done(((f32[512,512]{1,0:T(8,128)}), f32[512,512]{1,0:T(8,128)}) %all-reduce.4.cloned.1.call-update) | async-done | bytes 1048592 | tf_op jit(solution)/shard_map/psum | solution.py:52
  133.7 1.0 fusion.81
  134.6 4.3 %collective-permute-start = (f32[32,512]{1,0:T(8,128)S(1)}, f32[32,512]{1,0:T(8,128)S(1)}, u32[]{:S(2)}, u32[]{:S(2)}) collective-permute-start(f32[32,512]{1,0:T(8,128)S(1)} %get-tuple-element.23), channel_id=1, source_target_pairs={{0,16},{16,32},{32,48},{48,64},{64,80},{80,96},{96,112},{112,128},... | collective-permute-start | bytes 196616 | tf_op jit(solution)/shard_map/ppermute | solution.py:16
  139.0 1.3 collective-permute-start.1
  140.3 0.6 collective-permute-done
  140.8 1.5 constant_dynamic-update-slice_fusion
  142.3 5.1 %collective-permute-done.1 = f32[32,512]{1,0:T(8,128)S(1)} collective-permute-done((f32[32,512]{1,0:T(8,128)S(1)}, f32[32,512]{1,0:T(8,128)S(1)}, u32[]{:S(2)}, u32[]{:S(2)}) %collective-permute-start.1) | collective-permute-done | bytes 65568 | tf_op jit(solution)/shard_map/ppermute | solution.py:19
  147.5 12.3 %fusion.17 = f32[512,512]{1,0:T(8,128)S(1)} fusion(f32[544,512]{1,0:T(8,128)S(1)} %constant_dynamic-update-slice_fusion.2, f32[544,512]{1,0:T(8,128)S(1)} %get-tuple-element.21, f32[512,512]{1,0:T(8,128)S(1)} %copy-done.1, s32[512]{0:T(512)S(1)} %copy-done.5, s32[512]{0:T(512)S(1)} %iota_add_fusion, pred[512]{0:T(512)(128)(4,1)S(1)} %get-tuple-element.57, ...), kind=kLoop, calls=%fused_computation.33 | loop fusion | flops 36438016 | bytes 69227008 | tf_op jit(solution)/shard_map/rsqrt | solution.py:42
  160.3 3.1 dynamic-slice_select_fusion.3
  163.4 226.0 %all-reduce.6.cloned.1.call-done = (bf16[2,512,512]{2,1,0:T(8,128)(2,1)}, bf16[2,512,512]{2,1,0:T(8,128)(2,1)}, bf16[2,512,512]{2,1,0:T(8,128)(2,1)}, bf16[2,512,512]{2,1,0:T(8,128)(2,1)}) async-done(((bf16[2,512,512]{2,1,0:T(8,128)(2,1)}, bf16[2,512,512]{2,1,0:T(8,128)(2,1)}, bf16[2,512,512]{2,1,0:T(8,128)(2,1)}, bf16[2,512,512]{2,1,0:T(8,128)(2,1)}), (bf16[2,512,512]{2,1,0:T(8,128)(2,1)}, ...) | async-done | bytes 4194320 | tf_op jit(solution)/shard_map/psum | solution.py:26
  389.4 2.5 fusion.87
  392.2 0.9 copy-done.4
  393.1 1.3 fusion.86
  394.7 0.9 copy-done.3
  395.6 1.3 fusion.85
  397.2 0.9 copy-done.2
  398.2 1.3 fusion.84
  399.7 0.5 fusion.4
  400.3 0.5 fusion.2
  400.8 0.6 pad_maximum_fusion
  401.4 2.3 copy.5
  (26 shorter events, 1.7 us)
Async XLA Ops:
  6.5 3.2 copy-start.6
  6.5 8.8 %copy-start.7 = (s32[4]{0:T(128)S(1)}, s32[4]{0:T(128)}, u32[]{:S(2)}) copy-start(s32[4]{0:T(128)} %param.6) | copy-start | bytes 52
  6.5 14.5 %copy-start.5 = (s32[512]{0:T(512)S(1)}, s32[512]{0:T(512)}, u32[]{:S(2)}) copy-start(s32[512]{0:T(512)} %param.5) | copy-start | bytes 6148
  6.5 127.1 %all-reduce.4.cloned.1.call-start = ((), (), s32[]{:S(2)}) async-start(), calls=%async_computation | async-start | bytes 2097152 | tf_op jit(solution)/shard_map/psum | solution.py:52
  9.7 379.7 %all-reduce.6.cloned.1.call-start = ((), (), s32[]{:S(2)}) async-start(), calls=%async_computation.1 | async-start | bytes 8388608 | tf_op jit(solution)/shard_map/psum | solution.py:26
  133.7 13.8 %copy-start.1 = (f32[512,512]{1,0:T(8,128)S(1)}, f32[512,512]{1,0:T(8,128)}, u32[]{:S(2)}) copy-start(f32[512,512]{1,0:T(8,128)} %all-reduce.4.cloned.1.call-done) | copy-start | bytes 3145732
  134.6 6.2 %collective-permute-start = (f32[32,512]{1,0:T(8,128)S(1)}, f32[32,512]{1,0:T(8,128)S(1)}, u32[]{:S(2)}, u32[]{:S(2)}) collective-permute-start(f32[32,512]{1,0:T(8,128)S(1)} %get-tuple-element.23), channel_id=1, source_target_pairs={{0,16},{16,32},{32,48},{48,64},{64,80},{80,96},{96,112},{112,128},... | collective-permute-start | bytes 196616 | tf_op jit(solution)/shard_map/ppermute | solution.py:16
  139.0 8.5 %collective-permute-start.1 = (f32[32,512]{1,0:T(8,128)S(1)}, f32[32,512]{1,0:T(8,128)S(1)}, u32[]{:S(2)}, u32[]{:S(2)}) collective-permute-start(f32[32,512]{1,0:T(8,128)S(1)} %get-tuple-element.24), channel_id=1, source_target_pairs={{16,0},{32,16},{48,32},{64,48},{80,64},{96,80},{112,96},{128,112},... | collective-permute-start | bytes 196616 | tf_op jit(solution)/shard_map/ppermute | solution.py:19
  147.5 12.4 %copy-start = (bf16[2,2,512,512]{3,2,1,0:T(8,128)(2,1)S(1)}, bf16[2,2,512,512]{3,2,1,0:T(8,128)(2,1)}, u32[]{:S(2)}) copy-start(bf16[2,2,512,512]{3,2,1,0:T(8,128)(2,1)} %param.4) | copy-start | bytes 6291460
  391.9 1.2 copy-start.4
  394.4 1.2 copy-start.3
  396.9 1.2 copy-start.2
Sparse Core Ops, SparseCore 0:
  10.0 123.6 all-reduce.3
  163.5 225.8 all-reduce.5
where the time goes:
time: 411 us
  waiting for transfers between devices  344 us (84%)
  between operations  23.6 us (6%)
  other arithmetic  21.8 us (5%)
  local copies, waits for them, and re-layouts  8.92 us (2%)
  matrix products  6.34 us (2%)
  starting transfers between devices  5.63 us (1%)
    psum x1, waiting for transfers between devices, from_root(): return lax.psum(block, axis)  226 us
    psum x1, waiting for transfers between devices, local(): power = lax.psum(local_power, 'band')  113 us
    rsqrt x1, other arithmetic, norm_scale(): return lax.rsqrt(total / (count.astype(jnp.float32) * bins) + 1e-06)  12.3 us
  transfers between devices with their start and end apart: 4, of which 4 were waited for; matrix products, arithmetic and copies ran while one was open for 1% of the time, Pallas kernels for 0%

commit v1 on v0

v1 whole, which is shorter than its diff:
```python
import jax
import jax.numpy as jnp
from jax import lax
from jax.experimental import pallas as pl
from jax.experimental.pallas import tpu as pltpu
from jax.sharding import PartitionSpec as P

MESH = pl.DeviceIdType.MESH
PANEL = 256
NPANEL = 4
HALO = 32
ROWS = 512
WIN = 512
Q = 128
NX = 4
NZ = 4
NCHAN = 16
NBAND = 16
PLANES = 4
CHANNELS = ROWS * NCHAN
BINS = 32
F32 = jnp.float32
BF16 = jnp.bfloat16


def move_kernel(
    spec, width, block, offset, gath, means,
    a0, a1, a2, a3, b0, b1, b2, b3, picked, onehot, power, bands, total, ms, parts, sel, wide,
    a_s, a_r, rz_s, rz_r, gz_s, gz_r, gx_s, gx_r, e_s, e_r, rb_s, rb_r, rc_s, rc_r, gc_s, gc_r, gb_s, gb_r,
):
    c, b = lax.axis_index("chan"), lax.axis_index("band")
    x, z = c // NZ, c % NZ
    rq, wq = b // 4, b % 4
    a, zb = (a0, a1, a2, a3), (b0, b1, b2, b3)

    def at_x(d):
        return ((x + d) % NX * NZ + z, b)

    def at_z(d):
        return (x * NZ + (z + d) % NZ, b)

    def at_c(d):
        return ((c + d) % NCHAN, b)

    def at_b(d):
        return (c, (b + d) % NBAND)

    def send(src, dst, ssem, rsem, dev):
        copy = pltpu.make_async_remote_copy(
            src_ref=src, dst_ref=dst, send_sem=ssem, recv_sem=rsem, device_id=dev, device_id_type=MESH
        )
        copy.start()
        return copy

    barrier = pltpu.get_barrier_semaphore()
    for d in range(1, NCHAN):
        pl.semaphore_signal(barrier, inc=1, device_id=at_c(d), device_id_type=MESH)
    for d in range(1, NBAND):
        pl.semaphore_signal(barrier, inc=1, device_id=at_b(d), device_id_type=MESH)

    def local_power(lo, count):
        acc = jnp.zeros((count, WIN), F32)
        for f in range(2):
            for k in range(2):
                v = spec[f, k, pl.ds(lo, count), :].astype(F32)
                acc = acc + v * v
        power[pl.ds(lo + HALO, count), :] = acc.astype(BF16)

    local_power(0, HALO)
    local_power(ROWS - HALO, HALO)
    pl.semaphore_wait(barrier, NCHAN + NBAND - 2)

    pending = []

    a_cp = []
    for q in range(PLANES):
        f, k = q // 2, q % 2
        row = []
        for d in (1, 3, 2):
            cols = pl.ds(pl.multiple_of((x + d) % NX * Q, Q), Q)
            row.append(send(spec.at[f, k, :, cols], a[q].at[d], a_s.at[q, d], a_r.at[q, d], at_x(d)))
        a_cp.append(row)
    up = send(power.at[pl.ds(ROWS, HALO)], power.at[pl.ds(0, HALO)], e_s.at[0], e_r.at[0], at_c(1))
    down = send(
        power.at[pl.ds(HALO, HALO)], power.at[pl.ds(ROWS + HALO, HALO)], e_s.at[1], e_r.at[1], at_c(NCHAN - 1)
    )

    def body(i, carry):
        local_power(pl.multiple_of(i * HALO, HALO), HALO)
        return carry

    lax.fori_loop(1, ROWS // HALO - 1, body, 0)
    own_cols = pl.ds(pl.multiple_of(x * Q, Q), Q)
    for q in range(PLANES):
        a[q][0] = spec[q // 2, q % 2, :, own_cols]
    for p in range(NPANEL):
        here = lax.broadcasted_iota(jnp.int32, (PANEL, ROWS), 1)
        want = lax.broadcasted_iota(jnp.int32, (PANEL, ROWS), 0) + offset[p]
        onehot[p] = jnp.where(here == want, 1.0, 0.0).astype(BF16)

    up.wait_recv()
    down.wait_recv()
    rb = []
    for d in range(1, NBAND):
        t = (b + d) % NBAND
        src = power.at[pl.ds(pl.multiple_of(t // 4 * Q, Q), Q + 2 * HALO), pl.ds(pl.multiple_of(t % 4 * Q, Q), Q)]
        rb.append(send(src, bands.at[d], rb_s.at[d], rb_r.at[d], at_b(d)))
    pending += [up, down]

    def pick(q):
        for cp in a_cp[q]:
            cp.wait_recv()
        for p in range(NPANEL):
            slot = lax.rem(x - block[p] // NZ + NX, NX)
            picked[q, p] = jnp.dot(onehot[p], a[q][slot], preferred_element_type=F32).astype(BF16)
        zb[q][0] = picked[q, :, pl.ds(pl.multiple_of(z * 64, 64), 64), :]
        out = []
        for d in (1, 3, 2):
            rows = pl.ds(pl.multiple_of((z + d) % NZ * 64, 64), 64)
            out.append(send(picked.at[q, :, rows, :], zb[q].at[d], rz_s.at[q, d], rz_r.at[q, d], at_z(d)))
        return out

    own_rows = pl.ds(pl.multiple_of(z * 64, 64), 64)

    def share_z(q, copies):
        f, k = q // 2, q % 2
        for cp in copies:
            cp.wait_recv()
        for p in range(NPANEL):
            slot = lax.rem(z - block[p] % NZ + NZ, NZ)
            gath[f, p, k, own_rows, own_cols] = zb[q][slot, p]
        out = []
        for d in (1, 3, 2):
            part = gath.at[f, :, k, own_rows, own_cols]
            out.append(send(part, part, gz_s.at[q, d], gz_r.at[q, d], at_z(d)))
        return out

    def share_x(q, copies):
        f, k = q // 2, q % 2
        for cp in copies:
            cp.wait_recv()
        part = gath.at[f, :, k, :, own_cols]
        right = send(part, part, gx_s.at[q, 0], gx_r.at[q, 0], at_x(1))
        left = send(part, part, gx_s.at[q, 1], gx_r.at[q, 1], at_x(3))
        return [right, left]

    def pass_x(q, copies):
        f, k = q // 2, q % 2
        right, left = copies
        right.wait_recv()
        cols = pl.ds(pl.multiple_of((x + 3) % NX * Q, Q), Q)
        part = gath.at[f, pl.ds(0, 2), k, :, cols]
        on_right = send(part, part, gx_s.at[q, 2], gx_r.at[q, 2], at_x(1))
        left.wait_recv()
        cols = pl.ds(pl.multiple_of((x + 1) % NX * Q, Q), Q)
        part = gath.at[f, pl.ds(2, 2), k, :, cols]
        on_left = send(part, part, gx_s.at[q, 3], gx_r.at[q, 3], at_x(3))
        return [on_right, on_left]

    rz, gz, gx, fx = [None] * 4, [None] * 4, [None] * 4, [None] * 4
    rz[0] = pick(0)

    for cp in rb:
        cp.wait_recv()
    acc = power[
        pl.ds(pl.multiple_of(rq * Q, Q), Q + 2 * HALO), pl.ds(pl.multiple_of(wq * Q, Q), Q)
    ].astype(F32)
    for d in range(1, NBAND):
        acc = acc + bands[d].astype(F32)
    first = c * ROWS + rq * Q
    chan = lax.broadcasted_iota(jnp.int32, (Q + 2 * HALO, Q), 0) + (first - HALO)
    total[...] = jnp.where((chan >= 0) & (chan < CHANNELS), acc, 0.0)
    half = width[:, pl.ds(pl.multiple_of(wq * Q, Q), Q)]
    win = total[HALO : HALO + Q, :]
    for o in range(1, HALO + 1):
        both = total[HALO - o : HALO - o + Q, :] + total[HALO + o : HALO + o + Q, :]
        win = win + jnp.where(half >= o, both, 0.0)
    chan = lax.broadcasted_iota(jnp.int32, (Q, Q), 0) + first
    count = jnp.minimum(chan + half, CHANNELS - 1) - jnp.maximum(chan - half, 0) + 1
    mean = win / (count.astype(F32) * BINS) + 1e-6
    ms[...] = mean
    my_rows = pl.ds(pl.multiple_of(rq * Q, Q), Q)
    my_cols = pl.ds(pl.multiple_of(wq * Q, Q), Q)
    means[0, my_rows, my_cols] = mean.astype(BF16)
    rc = []
    for d in range(1, NCHAN):
        src = ms.at[pl.ds(pl.multiple_of((c + d) % NCHAN * 8, 8), 8)]
        rc.append(send(src, parts.at[d], rc_s.at[d], rc_r.at[d], at_c(d)))
    parts[0] = ms[pl.ds(pl.multiple_of(c * 8, 8), 8), :]

    rz[1] = pick(1)
    gz[0] = share_z(0, rz[0])

    for cp in rc:
        cp.wait_recv()
    sel[...] = jnp.concatenate([parts[lax.rem(c - block[p] + NCHAN, NCHAN)] for p in range(NPANEL)], axis=0).astype(BF16)
    gc = []
    for d in range(1, NCHAN):
        gc.append(send(sel, wide.at[c], gc_s.at[d], gc_r.at[d], at_c(d)))
    wide[c] = sel[...]

    rz[2] = pick(2)
    gz[1] = share_z(1, rz[1])
    gx[0] = share_x(0, gz[0])

    for cp in gc:
        cp.wait_recv()
    every = wide[...].astype(F32)
    for p in range(NPANEL):
        means[1 + p, my_rows, my_cols] = every[:, p * 8 : p * 8 + 8, :].reshape(Q, Q).astype(BF16)
    part = means.at[:, my_rows, my_cols]
    zl = send(part, part, gb_s.at[0], gb_r.at[0], at_b(8))

    rz[3] = pick(3)
    gz[2] = share_z(2, rz[2])
    gx[1] = share_x(1, gz[1])

    zl.wait_recv()
    far_rows = pl.ds(pl.multiple_of((rq + 2) % 4 * Q, Q), Q)
    gy = []
    for d in range(1, 4):
        t = (c, b // 8 * 8 + (b % 8 + 2 * d) % 8)
        for i, rows in enumerate((my_rows, far_rows)):
            part = means.at[:, rows, my_cols]
            gy.append(send(part, part, gb_s.at[2 * d + i], gb_r.at[2 * d + i], t))

    fx[0] = pass_x(0, gx[0])
    gz[3] = share_z(3, rz[3])
    gx[2] = share_x(2, gz[2])
    fx[1] = pass_x(1, gx[1])

    for cp in gy:
        cp.wait_recv()
    core = b % 2
    gk = []
    for i in range(2):
        part = means.at[:, :, pl.ds(pl.multiple_of((2 * i + core) * Q, Q), Q)]
        gk.append(send(part, part, gb_s.at[8 + i], gb_r.at[8 + i], (c, b // 2 * 2 + (b + 1) % 2)))

    gx[3] = share_x(3, gz[3])
    fx[2] = pass_x(2, gx[2])
    fx[3] = pass_x(3, gx[3])
    for cp in gk:
        cp.wait_recv()
    for q in range(PLANES):
        for cp in fx[q]:
            cp.wait_recv()
    for q in range(PLANES):
        pending += a_cp[q] + rz[q] + gz[q] + gx[q] + fx[q]
    for cp in pending + rb + rc + gc + [zl] + gy + gk:
        cp.wait_send()


def multiply_kernel(offset, spec, gath, means_own, means_panel, out, normed, scale):
    p, f = pl.program_id(0), pl.program_id(1)

    @pl.when(p == 0)
    def _():
        own = lax.rsqrt(means_own[0].astype(F32))
        re = (spec[0, 0].astype(F32) * own).astype(BF16)
        im = (spec[0, 1].astype(F32) * own).astype(BF16)
        normed[f, :ROWS, :WIN] = re
        normed[f, :ROWS, WIN:] = im
        normed[f, ROWS:, :WIN] = im
        normed[f, ROWS:, WIN:] = -re

    @pl.when(f == 0)
    def _():
        here = lax.broadcasted_iota(jnp.int32, (PANEL, ROWS), 1)
        want = lax.broadcasted_iota(jnp.int32, (PANEL, ROWS), 0) + offset[p]
        onehot = jnp.where(here == want, 1.0, 0.0).astype(BF16)
        scale[...] = lax.rsqrt(jnp.dot(onehot, means_panel[0], preferred_element_type=F32))

    right = jnp.concatenate([(gath[0, 0, k].astype(F32) * scale[...]).astype(BF16) for k in range(2)], axis=1)
    for k in range(2):
        gram = lax.dot_general(
            normed[f, k * ROWS : (k + 1) * ROWS, :], right, (((1,), (1,)), ((), ())), preferred_element_type=F32
        )
        out[0, 0, k] = (gram * WIN ** (-0.5)).astype(BF16)


def local(spectra, half_width, panel_block, panel_offset):
    dma = pltpu.SemaphoreType.DMA
    vmem = pl.BlockSpec(memory_space=pltpu.VMEM)
    smem = pl.BlockSpec(memory_space=pltpu.SMEM)
    gath, means = pl.pallas_call(
        move_kernel,
        out_shape=(
            jax.ShapeDtypeStruct((2, NPANEL, 2, PANEL, WIN), BF16),
            jax.ShapeDtypeStruct((1 + NPANEL, ROWS, WIN), BF16),
        ),
        in_specs=[vmem, vmem, smem, smem],
        out_specs=(vmem, vmem),
        scratch_shapes=[pltpu.VMEM((NX, ROWS, Q), BF16)] * 4
        + [pltpu.VMEM((NZ, NPANEL, 64, Q), BF16)] * 4
        + [
            pltpu.VMEM((PLANES, NPANEL, PANEL, Q), BF16),
            pltpu.VMEM((NPANEL, PANEL, ROWS), BF16),
            pltpu.VMEM((ROWS + 2 * HALO, WIN), BF16),
            pltpu.VMEM((NBAND, Q + 2 * HALO, Q), BF16),
            pltpu.VMEM((Q + 2 * HALO, Q), F32),
            pltpu.VMEM((Q, Q), F32),
            pltpu.VMEM((NCHAN, 8, Q), F32),
            pltpu.VMEM((32, Q), BF16),
            pltpu.VMEM((NCHAN, 32, Q), BF16),
        ]
        + [dma((4, 4))] * 8
        + [dma((2,))] * 2
        + [dma((16,))] * 6
        + [dma((10,))] * 2,
        compiler_params=pltpu.CompilerParams(
            collective_id=0, has_side_effects=True, vmem_limit_bytes=40 * 1024 * 1024
        ),
        name="move_panels_and_power",
    )(spectra, half_width[None, :], panel_block, panel_offset)
    return pl.pallas_call(
        multiply_kernel,
        out_shape=jax.ShapeDtypeStruct((NPANEL, 2, 2, ROWS, PANEL), BF16),
        grid=(NPANEL, 2),
        in_specs=[
            smem,
            pl.BlockSpec((1, 2, ROWS, WIN), lambda p, f: (jnp.where(p == 0, f, 1), 0, 0, 0)),
            pl.BlockSpec((1, 1, 2, PANEL, WIN), lambda p, f: (f, p, 0, 0, 0)),
            pl.BlockSpec((1, ROWS, WIN), lambda p, f: (0, 0, 0)),
            pl.BlockSpec((1, ROWS, WIN), lambda p, f: (1 + p, 0, 0)),
        ],
        out_specs=pl.BlockSpec((1, 1, 2, ROWS, PANEL), lambda p, f: (p, f, 0, 0, 0)),
        scratch_shapes=[pltpu.VMEM((2, 2 * ROWS, 2 * WIN), BF16), pltpu.VMEM((PANEL, WIN), F32)],
        compiler_params=pltpu.CompilerParams(vmem_limit_bytes=40 * 1024 * 1024),
        name="normalize_and_multiply",
    )(panel_offset, spectra, gath, means, means)


def solution(mesh):
    placed = (P("band", None, "chan", None), P(), P(), P())
    return jax.shard_map(
        local,
        mesh=mesh,
        in_specs=placed,
        out_specs=P(None, "band", None, "chan", None),
        check_vma=False,
    )
```

time: 411 us -> 112 us (0.27)
  waiting for transfers between devices: 344 us -> 0 us
  Pallas kernels: 0 us -> 107 us
  between operations: 23.6 us -> 0.01 us
  other arithmetic: 21.8 us -> 0 us
  matrix products: 6.34 us -> 0 us
  starting transfers between devices: 5.63 us -> 0 us
  local copies, waits for them, and re-layouts: 8.92 us -> 3.58 us
    psum x2 -> x0, waiting for transfers between devices: 339 us -> none  [the longest x1 226 us: from_root(): return lax.psum(block, axis)]
    pallas_call x0 -> x2, Pallas kernels: none -> 107 us  [the longest x1 97.7 us: local(): pl.pallas_call(move_kernel, out_shape=(jax.ShapeDtypeStruct((2, NPANEL, 2...]
    rsqrt x1 -> x0, other arithmetic: 12.3 us -> none  [norm_scale(): return lax.rsqrt(total / (count.astype(jnp.float32) * bins) + 1e-06)]
    dot_general x4 -> x0, matrix products: 6.34 us -> none  [local(): jnp.einsum('fxw,fyw->fxy', flat, right, preferred_element_type=jnp.float32)]
    ppermute x2 -> x0, waiting for transfers between devices: 5.71 us -> none  [the longest x1 5.14 us: with_halo(): lax.ppermute(lax.slice_in_dim(block, 0, width, axis=dim), axis, backward)]
    ppermute x2 -> x0, starting transfers between devices: 5.59 us -> none  [the longest x1 4.3 us: with_halo(): lax.ppermute(lax.slice_in_dim(block, block.shape[dim] - width, None, axis...]
  transfers between devices with their start and end apart: 4 -> 0, of which waited for: 4 -> 0; matrix products, arithmetic and copies ran while one was open for 1% -> 0% of each run, Pallas kernels for 0% -> 0%
where the time goes in v1:
time: 112 us; the launch traced here: 111 us
  Pallas kernels  107 us (96%)
  local copies, waits for them, and re-layouts  3.58 us (3%)
    pallas_call x1, Pallas kernels, local(): pl.pallas_call(move_kernel, out_shape=(jax.ShapeDtypeStruct((2, NPANEL, 2...  97.7 us
    pallas_call x1, Pallas kernels, local(): pl.pallas_call(multiply_kernel, out_shape=jax.ShapeDtypeStruct((NPANEL, 2...  9.72 us
    unnamed x8, local copies, waits for them, and re-layouts  3.58 us

profile of v1, /device:TPU:8, one launch (start us, length us, event | category | flops | bytes accessed | tf_op | source)
XLA Modules:
  0.0 111.0 jit_solution(3365078062698584130)
XLA Ops:
  0.0 0.0 copy-start
  0.0 1.6 %copy-done = bf16[2,2,512,512]{3,2,1,0:T(8,128)(2,1)S(1)} copy-done((bf16[2,2,512,512]{3,2,1,0:T(8,128)(2,1)S(1)}, bf16[2,2,512,512]{3,2,1,0:T(8,128)(2,1)}, u32[]{:S(2)}) %copy-start) | copy-done | bytes 2097176
  1.6 0.0 copy-start.1
  1.6 0.7 copy-done.1
  2.2 0.0 copy-start.2
  2.2 0.7 copy-done.2
  2.9 0.0 copy-start.3
  2.9 0.7 copy-done.3
  3.6 97.7 %move_panels_and_power.1 = (bf16[2,4,2,256,512]{4,3,2,1,0:T(8,128)(2,1)S(1)}, bf16[5,512,512]{2,1,0:T(8,128)(2,1)S(1)}) custom-call(bf16[2,2,512,512]{3,2,1,0:T(8,128)(2,1)S(1)} %copy-done, s32[1,512]{1,0:T(1,128)S(1)} %bitcast.1, s32[4]{0:T(128)S(1)} %copy-done.3, s32[4]{0:T(128)S(1)} %copy-done.1), custom_call_target="tpu_custom_call" | custom-call | tf_op jit(solution)/shard_map/move_panels_and_power/pallas_call | solution.py:286
  101.3 9.7 %normalize_and_multiply.1 = bf16[4,2,2,512,256]{4,3,2,1,0:T(8,128)(2,1)} custom-call(s32[4]{0:T(128)S(1)} %copy-done.1, bf16[2,2,512,512]{3,2,1,0:T(8,128)(2,1)S(1)} %copy-done, bf16[2,4,2,256,512]{4,3,2,1,0:T(8,128)(2,1)S(1)} %get-tuple-element.7.gath, bf16[5,512,512]{2,1,0:T(8,128)(2,1)S(1)} %get-tuple-element.8.means_own.means_panel, ...), custom_call_target="tpu_custom_call" | custom-call | tf_op jit(solution)/shard_map/normalize_and_multiply/pallas_call | solution.py:316
Async XLA Ops:
  0.0 1.6 %copy-start = (bf16[2,2,512,512]{3,2,1,0:T(8,128)(2,1)S(1)}, bf16[2,2,512,512]{3,2,1,0:T(8,128)(2,1)}, u32[]{:S(2)}) copy-start(bf16[2,2,512,512]{3,2,1,0:T(8,128)(2,1)} %spec.3) | copy-start | bytes 6291460
  1.6 0.7 copy-start.1
  2.2 0.7 copy-start.2
  2.9 0.7 copy-start.3

commit v2 on v0

v2 whole, which is shorter than its diff:
```python
import jax
import jax.numpy as jnp
from jax import lax
from jax.experimental import pallas as pl
from jax.experimental.pallas import tpu as pltpu
from jax.sharding import PartitionSpec as P

MESH = pl.DeviceIdType.MESH
PANEL = 256
NPANEL = 4
HALO = 32
ROWS = 512
WIN = 512
Q = 128
R = 64
NX = 4
NZ = 4
NCHAN = 16
NBAND = 16
PLANES = 4
CHANNELS = ROWS * NCHAN
BINS = 32
WB = WIN // NBAND
F32 = jnp.float32
BF16 = jnp.bfloat16

PLAN = (
    ("pick", 0), ("pick", 2), ("band_sum", 0), ("pick", 3), ("window", 0), ("share_z", 2), ("pick", 1), ("own_y", 0),
    ("share_z", 0), ("pass_z", 2), ("share_z", 3), ("pass_z", 0), ("pick", 4), ("share_x", 2), ("choose", 0),
    ("pass_z", 3), ("own_core", 0), ("share_z", 1), ("share_x", 0), ("gathered", 0), ("pick", 6), ("share_z", 4),
    ("share_x", 3), ("pass_z", 1), ("pass_x", 2), ("pass_x", 3), ("panel_y", 0), ("share_z", 6), ("pass_x", 0),
    ("pass_z", 4), ("pick", 7), ("share_x", 1), ("share_x", 4), ("pass_z", 6), ("pick", 5), ("own_norm", 0),
    ("panel_core", 0), ("share_z", 7), ("share_x", 6), ("pass_x", 1), ("share_z", 5), ("pass_x", 4), ("pass_z", 7),
    ("own_norm", 1), ("pass_x", 6), ("pass_z", 5), ("share_x", 7), ("panel_scale", 0), ("share_x", 5),
    ("multiply", 2), ("pass_x", 7), ("multiply", 1), ("pass_x", 5), ("multiply", 0), ("multiply", 3),
)


def root(fourth):
    return lax.rsqrt(jnp.sqrt(jnp.sqrt(fourth)))


def move_kernel(
    spec_hbm, width_hbm, block_hbm, offset_hbm, out_hbm,
    spec, width, block, offset, a0, a1, a2, a3, b0, b1, b2, b3, b4, b5, b6, b7, gath, picked, onehot, power, bands, total,
    cand, parts, means, scale, left, out, l_s, o_s, a_s, a_r, rz_s, rz_r, gz_s, gz_r, gx_s, gx_r, e_s, e_r, rb_s, rb_r, rc_s, rc_r, gc_s, gc_r, gb_s, gb_r,
):
    c, b = lax.axis_index("chan"), lax.axis_index("band")
    x, z = c // NZ, c % NZ
    core = b % 2
    half_band = b // 2
    wb = core * 8 + half_band
    a, zb = (a0, a1, a2, a3), (b0, b1, b2, b3, b4, b5, b6, b7)

    def at_x(d):
        return ((x + d) % NX * NZ + z, b)

    def at_z(d):
        return (x * NZ + (z + d) % NZ, b)

    def at_c(d):
        return ((c + d) % NCHAN, b)

    def at_b(d):
        return (c, (b + d) % NBAND)

    def block_of(i, size, count=None):
        return pl.ds(pl.multiple_of(i * size, size), count or size)

    def send(src, dst, ssem, rsem, dev):
        copy = pltpu.make_async_remote_copy(
            src_ref=src, dst_ref=dst, send_sem=ssem, recv_sem=rsem, device_id=dev, device_id_type=MESH
        )
        copy.start()
        return copy

    loads = [
        pltpu.make_async_copy(src, dst, l_s.at[i])
        for i, (src, dst) in enumerate(
            ((spec_hbm, spec), (width_hbm, width), (block_hbm, block), (offset_hbm, offset))
        )
    ]
    for cp in loads:
        cp.start()
    barrier = pltpu.get_barrier_semaphore()
    for d in range(1, NCHAN):
        pl.semaphore_signal(barrier, inc=1, device_id=at_c(d), device_id_type=MESH)
    for d in range(1, NBAND):
        pl.semaphore_signal(barrier, inc=1, device_id=at_b(d), device_id_type=MESH)
    pl.semaphore_wait(barrier, NCHAN + NBAND - 2)

    a_cp = [None] * PLANES
    for q in range(PLANES):
        f, k = q // 2, q % 2
        a_cp[q] = []
        for d in (1, 3, 2):
            cols = block_of((x + d) % NX, Q)
            a_cp[q].append(send(spec_hbm.at[f, k, :, cols], a[q].at[d], a_s.at[q, d], a_r.at[q, d], at_x(d)))

    for cp in loads:
        cp.wait()
    for i in range(ROWS // Q):
        acc = jnp.zeros((Q, WIN), F32)
        for f in range(2):
            for k in range(2):
                v = spec[f, k, i * Q : (i + 1) * Q, :].astype(F32)
                acc = acc + v * v
        for j in range(WIN // Q):
            power[j * Q : (j + 1) * Q, i * Q : (i + 1) * Q] = acc[:, j * Q : (j + 1) * Q].T.astype(BF16)
    rb = []
    for d in range(1, NBAND):
        t = (b + d) % NBAND
        src = power.at[block_of(t % 2 * 8 + t // 2, WB), :]
        rb.append(send(src, bands.at[d], rb_s.at[d], rb_r.at[d], at_b(d)))

    for q in range(PLANES):
        a[q][0] = spec[q // 2, q % 2, :, block_of(x, Q)]
    for p in range(NPANEL):
        here = lax.broadcasted_iota(jnp.int32, (PANEL, ROWS), 1)
        want = lax.broadcasted_iota(jnp.int32, (PANEL, ROWS), 0) + offset[p]
        onehot[p] = jnp.where(here == want, 1.0, 0.0).astype(BF16)

    st = {"rb": rb}

    def wait(name):
        for cp in st[name]:
            cp.wait_recv()

    arrived = set()

    def pick(u):
        q, h = u // 2, u % 2
        if q not in arrived:
            arrived.add(q)
            for cp in a_cp[q]:
                cp.wait_recv()
        for p in (2 * h, 2 * h + 1):
            slot = lax.rem(x - block[p] // NZ + NX, NX)
            picked[q, p] = jnp.dot(onehot[p], a[q][slot], preferred_element_type=F32).astype(BF16)
        zb[u][0] = picked[q, 2 * h : 2 * h + 2, block_of(z, R), :]
        st["rz", u] = []
        for d in (1, 3, 2):
            src = picked.at[q, pl.ds(2 * h, 2), block_of((z + d) % NZ, R), :]
            st["rz", u].append(send(src, zb[u].at[d], rz_s.at[u, d], rz_r.at[u, d], at_z(d)))

    def share_z(u):
        q, h = u // 2, u % 2
        wait(("rz", u))
        for i in range(2):
            slot = lax.rem(z - block[2 * h + i] % NZ + NZ, NZ)
            gath[q // 2, 2 * h + i, q % 2, block_of(z, R), block_of(x, Q)] = zb[u][slot, i]
        part = gath.at[q // 2, pl.ds(2 * h, 2), q % 2, block_of(z, R), block_of(x, Q)]
        st["gz", u] = [send(part, part, gz_s.at[u, i], gz_r.at[u, i], at_z(d)) for i, d in enumerate((1, 3))]

    def pass_z(u):
        q, h = u // 2, u % 2
        st["fz", u] = []
        for i, (came, to) in enumerate(((3, 1), (1, 3))):
            st["gz", u][i].wait_recv()
            part = gath.at[q // 2, 2 * h + i, q % 2, block_of((z + came) % NZ, R), block_of(x, Q)]
            st["fz", u].append(send(part, part, gz_s.at[u, 2 + i], gz_r.at[u, 2 + i], at_z(to)))

    def share_x(u):
        q, h = u // 2, u % 2
        wait(("fz", u))
        part = gath.at[q // 2, pl.ds(2 * h, 2), q % 2, :, block_of(x, Q)]
        st["gx", u] = [send(part, part, gx_s.at[u, i], gx_r.at[u, i], at_x(d)) for i, d in enumerate((1, 3))]

    def pass_x(u):
        q, h = u // 2, u % 2
        st["fx", u] = []
        for i, (came, to) in enumerate(((3, 1), (1, 3))):
            st["gx", u][i].wait_recv()
            part = gath.at[q // 2, 2 * h + i, q % 2, :, block_of((x + came) % NX, Q)]
            st["fx", u].append(send(part, part, gx_s.at[u, 2 + i], gx_r.at[u, 2 + i], at_x(to)))

    mine = block_of(wb, WB)
    across = block_of(core * 8 + (half_band + 4) % 8, WB)
    own_lanes, panel_lanes = pl.ds(0, ROWS), pl.ds(ROWS, NPANEL * PANEL)

    def band_sum(_):
        wait("rb")
        acc = power[mine, :].astype(F32)
        for d in range(1, NBAND):
            acc = acc + bands[d].astype(F32)
        total[:, Q : Q + ROWS] = acc
        st["e"] = [
            send(total.at[:, pl.ds(ROWS, Q)], total.at[:, pl.ds(0, Q)], e_s.at[0], e_r.at[0], at_c(1)),
            send(total.at[:, pl.ds(Q, Q)], total.at[:, pl.ds(ROWS + Q, Q)], e_s.at[1], e_r.at[1], at_c(NCHAN - 1)),
        ]

    def window(_):
        wait("e")
        wide = ROWS + 2 * Q
        chan = lax.broadcasted_iota(jnp.int32, (WB, wide), 1) + (c * ROWS - Q)
        ext = jnp.where((chan >= 0) & (chan < CHANNELS), total[...], 0.0)
        row = lax.broadcasted_iota(jnp.int32, (WB, ROWS), 0)
        half = jnp.zeros((WB, ROWS), jnp.int32)
        for i in range(WB):
            half = jnp.where(row == i, width[wb * WB + i], half)
        win = ext[:, Q : Q + ROWS]
        for o in range(1, HALO + 1):
            both = pltpu.roll(ext, o, 1) + pltpu.roll(ext, wide - o, 1)
            win = win + jnp.where(half >= o, both[:, Q : Q + ROWS], 0.0)
        chan = lax.broadcasted_iota(jnp.int32, (WB, ROWS), 1) + c * ROWS
        count = jnp.minimum(chan + half, CHANNELS - 1) - jnp.maximum(chan - half, 0) + 1
        mean = win / (count.astype(F32) * BINS) + 1e-6
        mean = ((mean * mean) * (mean * mean)).astype(BF16)
        means[mine, own_lanes] = mean
        part = means.at[mine, own_lanes]
        st["oz"] = [send(part, part, gb_s.at[0], gb_r.at[0], at_b(8))]
        for p in range(NPANEL):
            cand[:, p * PANEL : (p + 1) * PANEL] = lax.dot_general(
                mean, onehot[p], (((1,), (1,)), ((), ())), preferred_element_type=F32
            ).astype(BF16)
        st["rc"] = []
        for d in range(1, NCHAN):
            t = (c + d) % NCHAN
            src = cand.at[block_of(t % 2, 16), block_of(t // 2, Q)]
            st["rc"].append(send(src, parts.at[d], rc_s.at[d], rc_r.at[d], at_c(d)))
        parts[0] = cand[block_of(c % 2, 16), block_of(c // 2, Q)]

    def choose(_):
        wait("rc")
        mine_too = means.at[pl.ds(pl.multiple_of(wb * WB + c % 2 * 16, 16), 16), pl.ds(pl.multiple_of(ROWS + c // 2 * Q, Q), Q)]
        mine_too[...] = parts[lax.rem(c - block[c // 4] + NCHAN, NCHAN)]
        st["gc"] = [send(mine_too, mine_too, gc_s.at[d], gc_r.at[d], at_c(d)) for d in range(1, NCHAN)]

    def gathered(_):
        wait("gc")
        part = means.at[mine, panel_lanes]
        st["pz"] = [send(part, part, gb_s.at[8], gb_r.at[8], at_b(8))]

    def along_y(here, there, lanes, sem):
        wait(here)
        st[there] = []
        for d in range(1, 4):
            t = (c, b // 8 * 8 + (b % 8 + 2 * d) % 8)
            for i, rows in enumerate((mine, across)):
                part = means.at[rows, lanes]
                s = sem + 2 * d - 1 + i
                st[there].append(send(part, part, gb_s.at[s], gb_r.at[s], t))

    def to_core(here, there, lanes, sem):
        wait(here)
        part = means.at[block_of(core, WIN // 2), lanes]
        st[there] = [send(part, part, gb_s.at[sem], gb_r.at[sem], (c, half_band * 2 + (core + 1) % 2))]

    def own_norm(half):
        if half == 0:
            wait("ok")
        for i in range(2 * half, 2 * half + 2):
            for j in range(WIN // Q):
                s = root(means[j * Q : (j + 1) * Q, i * Q : (i + 1) * Q].astype(F32)).T
                for f in range(2):
                    for k in range(2):
                        v = spec[f, k, i * Q : (i + 1) * Q, j * Q : (j + 1) * Q].astype(F32)
                        left[f, i * Q : (i + 1) * Q, k * WIN + j * Q : k * WIN + (j + 1) * Q] = (v * s).astype(BF16)

    def panel_scale(_):
        wait("pk")
        for p in range(NPANEL):
            for i in range(PANEL // Q):
                lanes = slice(ROWS + p * PANEL + i * Q, ROWS + p * PANEL + (i + 1) * Q)
                for j in range(WIN // Q):
                    scale[p, i * Q : (i + 1) * Q, j * Q : (j + 1) * Q] = root(
                        means[j * Q : (j + 1) * Q, lanes].astype(F32)
                    ).T

    stores = []

    def multiply(v):
        f, h = v // 2, v % 2
        wait(("fx", 4 * f + h))
        wait(("fx", 4 * f + 2 + h))

        def body(p, carry):
            re = (gath[f, p, 0].astype(F32) * scale[p]).astype(BF16)
            im = (gath[f, p, 1].astype(F32) * scale[p]).astype(BF16)
            for k, right in enumerate((jnp.concatenate([re, im], axis=1), jnp.concatenate([-im, re], axis=1))):
                gram = lax.dot_general(left[f], right, (((1,), (1,)), ((), ())), preferred_element_type=F32)
                out[p, f, k] = (gram * WIN ** (-0.5)).astype(BF16)
            return carry

        lax.fori_loop(2 * h, 2 * h + 2, body, 0)
        stores.append(pltpu.make_async_copy(out.at[pl.ds(2 * h, 2), f], out_hbm.at[pl.ds(2 * h, 2), f], o_s.at[v]))
        stores[-1].start()

    steps = {
        "pick": pick, "share_z": share_z, "pass_z": pass_z, "share_x": share_x, "pass_x": pass_x, "multiply": multiply,
        "band_sum": band_sum, "window": window, "choose": choose, "gathered": gathered,
        "own_y": lambda _: along_y("oz", "oy", own_lanes, 0),
        "own_core": lambda _: to_core("oy", "ok", own_lanes, 7),
        "panel_y": lambda _: along_y("pz", "py", panel_lanes, 8),
        "panel_core": lambda _: to_core("py", "pk", panel_lanes, 15),
        "own_norm": own_norm, "panel_scale": panel_scale,
    }
    for name, q in PLAN:
        steps[name](q)
    for group in a_cp + list(st.values()):
        for cp in group:
            cp.wait_send()
    for cp in stores:
        cp.wait()


def local(spectra, half_width, panel_block, panel_offset):
    dma = pltpu.SemaphoreType.DMA
    hbm = pl.BlockSpec(memory_space=pltpu.HBM)
    return pl.pallas_call(
        move_kernel,
        out_shape=jax.ShapeDtypeStruct((NPANEL, 2, 2, ROWS, PANEL), BF16),
        in_specs=[hbm] * 4,
        out_specs=hbm,
        scratch_shapes=[
            pltpu.VMEM((2, 2, ROWS, WIN), BF16),
            pltpu.SMEM((WIN,), jnp.int32),
            pltpu.SMEM((NPANEL,), jnp.int32),
            pltpu.SMEM((NPANEL,), jnp.int32),
        ]
        + [pltpu.VMEM((NX, ROWS, Q), BF16)] * 4
        + [pltpu.VMEM((NZ, 2, R, Q), BF16)] * 8
        + [
            pltpu.VMEM((2, NPANEL, 2, PANEL, WIN), BF16),
            pltpu.VMEM((PLANES, NPANEL, PANEL, Q), BF16),
            pltpu.VMEM((NPANEL, PANEL, ROWS), BF16),
            pltpu.VMEM((WIN, ROWS), BF16),
            pltpu.VMEM((NBAND, WB, ROWS), BF16),
            pltpu.VMEM((WB, ROWS + 2 * Q), F32),
            pltpu.VMEM((WB, NPANEL * PANEL), BF16),
            pltpu.VMEM((NCHAN, 16, Q), BF16),
            pltpu.VMEM((WIN, ROWS + NPANEL * PANEL), BF16),
            pltpu.VMEM((NPANEL, PANEL, WIN), F32),
            pltpu.VMEM((2, ROWS, 2 * WIN), BF16),
            pltpu.VMEM((NPANEL, 2, 2, ROWS, PANEL), BF16),
            dma((4,)),
            dma((4,)),
        ]
        + [dma((4, 4))] * 2
        + [dma((8, 4))] * 6
        + [dma((2,))] * 2
        + [dma((16,))] * 8,
        compiler_params=pltpu.CompilerParams(
            collective_id=0, has_side_effects=True, vmem_limit_bytes=60 * 1024 * 1024
        ),
        name="cross_spectra",
    )(spectra, half_width, panel_block, panel_offset)


def solution(mesh):
    placed = (P("band", None, "chan", None), P(), P(), P())
    return jax.shard_map(
        local,
        mesh=mesh,
        in_specs=placed,
        out_specs=P(None, "band", None, "chan", None),
        check_vma=False,
    )
```

time: 411 us -> 100 us (0.24)
  waiting for transfers between devices: 344 us -> 0 us
  Pallas kernels: 0 us -> 95.3 us
  between operations: 23.6 us -> 0.01 us
  other arithmetic: 21.8 us -> 0 us
  matrix products: 6.34 us -> 0 us
  starting transfers between devices: 5.63 us -> 0 us
  local copies, waits for them, and re-layouts: 8.92 us -> 4.57 us
    psum x2 -> x0, waiting for transfers between devices: 339 us -> none  [the longest x1 226 us: from_root(): return lax.psum(block, axis)]
    pallas_call x0 -> x1, Pallas kernels: none -> 95.3 us  [local(): pl.pallas_call(move_kernel, out_shape=jax.ShapeDtypeStruct((NPANEL, 2, 2,...]
    rsqrt x1 -> x0, other arithmetic: 12.3 us -> none  [norm_scale(): return lax.rsqrt(total / (count.astype(jnp.float32) * bins) + 1e-06)]
    dot_general x4 -> x0, matrix products: 6.34 us -> none  [local(): jnp.einsum('fxw,fyw->fxy', flat, right, preferred_element_type=jnp.float32)]
    ppermute x2 -> x0, waiting for transfers between devices: 5.71 us -> none  [the longest x1 5.14 us: with_halo(): lax.ppermute(lax.slice_in_dim(block, 0, width, axis=dim), axis, backward)]
    ppermute x2 -> x0, starting transfers between devices: 5.59 us -> none  [the longest x1 4.3 us: with_halo(): lax.ppermute(lax.slice_in_dim(block, block.shape[dim] - width, None, axis...]
  transfers between devices with their start and end apart: 4 -> 0, of which waited for: 4 -> 0; matrix products, arithmetic and copies ran while one was open for 1% -> 0% of each run, Pallas kernels for 0% -> 0%
where the time goes in v2:
time: 100 us; the launch traced here: 99.9 us
  Pallas kernels  95.3 us (95%)
  local copies, waits for them, and re-layouts  4.57 us (5%)
    pallas_call x1, Pallas kernels, local(): pl.pallas_call(move_kernel, out_shape=jax.ShapeDtypeStruct((NPANEL, 2, 2,...  95.3 us
    unnamed x1, local copies, waits for them, and re-layouts  4.57 us

profile of v2, /device:TPU:8, one launch (start us, length us, event | category | flops | bytes accessed | tf_op | source)
XLA Modules:
  0.0 99.9 jit_solution(7494214848324428105)
XLA Ops:
  0.0 95.3 %cross_spectra.1 = bf16[4,2,2,512,256]{4,3,2,1,0:T(8,128)(2,1)} custom-call(bf16[2,2,512,512]{3,2,1,0:T(8,128)(2,1)} %spec_hbm.1, s32[512]{0:T(512)} %width_hbm.1, s32[4]{0:T(128)} %block_hbm.1, s32[4]{0:T(128)} %offset_hbm.1), custom_call_target="tpu_custom_call" | custom-call | tf_op jit(solution)/shard_map/cross_spectra/pallas_call | solution.py:310
  95.3 4.6 %copy.6 = bf16[4,2,2,512,256]{4,3,2,1,0:T(8,128)(2,1)} copy(bf16[4,2,2,512,256]{4,3,2,1,0:T(8,128)(2,1)} %cross_spectra.1) | data formatting | bytes 8388608

commit v3 on v2

--- a/solution.py
+++ b/solution.py
@@ -25,14 +25,15 @@
 BF16 = jnp.bfloat16
 
 PLAN = (
-    ("pick", 0), ("pick", 2), ("band_sum", 0), ("pick", 3), ("window", 0), ("share_z", 2), ("pick", 1), ("own_y", 0),
-    ("share_z", 0), ("pass_z", 2), ("share_z", 3), ("pass_z", 0), ("pick", 4), ("share_x", 2), ("choose", 0),
-    ("pass_z", 3), ("own_core", 0), ("share_z", 1), ("share_x", 0), ("gathered", 0), ("pick", 6), ("share_z", 4),
-    ("share_x", 3), ("pass_z", 1), ("pass_x", 2), ("pass_x", 3), ("panel_y", 0), ("share_z", 6), ("pass_x", 0),
-    ("pass_z", 4), ("pick", 7), ("share_x", 1), ("share_x", 4), ("pass_z", 6), ("pick", 5), ("own_norm", 0),
-    ("panel_core", 0), ("share_z", 7), ("share_x", 6), ("pass_x", 1), ("share_z", 5), ("pass_x", 4), ("pass_z", 7),
-    ("own_norm", 1), ("pass_x", 6), ("pass_z", 5), ("share_x", 7), ("panel_scale", 0), ("share_x", 5),
-    ("multiply", 2), ("pass_x", 7), ("multiply", 1), ("pass_x", 5), ("multiply", 0), ("multiply", 3),
+    ("raw", 0), ("power", 0), ("prepare", 0), ("pick", 1), ("raw", 3), ("band_sum", 0), ("pick", 0), ("raw", 1),
+    ("raw", 2), ("share_z", 1), ("pick", 6), ("window", 0), ("pass_z", 1), ("pick", 2), ("share_z", 0),
+    ("share_z", 6), ("share_x", 1), ("share_z", 2), ("pick", 4), ("pass_z", 6), ("pass_x", 1), ("choose", 0),
+    ("pass_z", 0), ("own_y", 0), ("share_z", 4), ("pass_z", 2), ("share_x", 6), ("gathered", 0), ("pick", 7),
+    ("share_x", 0), ("panel_y", 0), ("pass_z", 4), ("share_x", 2), ("pick", 3), ("share_z", 7),
+    ("share_x", 4), ("pick", 5), ("pass_x", 2), ("pass_x", 6), ("panel_core", 0), ("pass_x", 0), ("pass_z", 7),
+    ("own_core", 0), ("share_z", 3), ("share_z", 5), ("pass_x", 4), ("share_x", 7), ("pass_z", 3), ("panel_scale", 0),
+    ("pass_z", 5), ("share_x", 3), ("own_norm", 0), ("share_x", 5), ("own_norm", 1), ("multiply", 2), ("pass_x", 3),
+    ("pass_x", 7), ("multiply", 0), ("pass_x", 5), ("multiply", 1), ("multiply", 3),
 )
 
 
@@ -49,7 +50,11 @@
     x, z = c // NZ, c % NZ
     core = b % 2
     half_band = b // 2
-    wb = core * 8 + half_band
+
+    def windows_of(t):
+        return t % 2 * 8 + t // 2 % 4 * 2 + t // 8
+
+    wb = windows_of(b)
     a, zb = (a0, a1, a2, a3), (b0, b1, b2, b3, b4, b5, b6, b7)
 
     def at_x(d):
@@ -90,37 +95,38 @@
     pl.semaphore_wait(barrier, NCHAN + NBAND - 2)
 
     a_cp = [None] * PLANES
-    for q in range(PLANES):
-        f, k = q // 2, q % 2
+
+    def raw(q):
         a_cp[q] = []
         for d in (1, 3, 2):
-            cols = block_of((x + d) % NX, Q)
-            a_cp[q].append(send(spec_hbm.at[f, k, :, cols], a[q].at[d], a_s.at[q, d], a_r.at[q, d], at_x(d)))
-
-    for cp in loads:
-        cp.wait()
-    for i in range(ROWS // Q):
-        acc = jnp.zeros((Q, WIN), F32)
-        for f in range(2):
-            for k in range(2):
-                v = spec[f, k, i * Q : (i + 1) * Q, :].astype(F32)
-                acc = acc + v * v
-        for j in range(WIN // Q):
-            power[j * Q : (j + 1) * Q, i * Q : (i + 1) * Q] = acc[:, j * Q : (j + 1) * Q].T.astype(BF16)
-    rb = []
-    for d in range(1, NBAND):
-        t = (b + d) % NBAND
-        src = power.at[block_of(t % 2 * 8 + t // 2, WB), :]
-        rb.append(send(src, bands.at[d], rb_s.at[d], rb_r.at[d], at_b(d)))
-
-    for q in range(PLANES):
-        a[q][0] = spec[q // 2, q % 2, :, block_of(x, Q)]
-    for p in range(NPANEL):
-        here = lax.broadcasted_iota(jnp.int32, (PANEL, ROWS), 1)
-        want = lax.broadcasted_iota(jnp.int32, (PANEL, ROWS), 0) + offset[p]
-        onehot[p] = jnp.where(here == want, 1.0, 0.0).astype(BF16)
-
-    st = {"rb": rb}
+            src = spec_hbm.at[q // 2, q % 2, :, block_of((x + d) % NX, Q)]
+            a_cp[q].append(send(src, a[q].at[d], a_s.at[q, d], a_r.at[q, d], at_x(d)))
+
+    def own_power(_):
+        for cp in loads:
+            cp.wait()
+        for i in range(ROWS // Q):
+            acc = jnp.zeros((Q, WIN), F32)
+            for f in range(2):
+                for k in range(2):
+                    v = spec[f, k, i * Q : (i + 1) * Q, :].astype(F32)
+                    acc = acc + v * v
+            for j in range(WIN // Q):
+                power[j * Q : (j + 1) * Q, i * Q : (i + 1) * Q] = acc[:, j * Q : (j + 1) * Q].T.astype(BF16)
+        st["rb"] = []
+        for d in range(1, NBAND):
+            src = power.at[block_of(windows_of((b + d) % NBAND), WB), :]
+            st["rb"].append(send(src, bands.at[d], rb_s.at[d], rb_r.at[d], at_b(d)))
+
+    def prepare(_):
+        for q in range(PLANES):
+            a[q][0] = spec[q // 2, q % 2, :, block_of(x, Q)]
+        for p in range(NPANEL):
+            here = lax.broadcasted_iota(jnp.int32, (PANEL, ROWS), 1)
+            want = lax.broadcasted_iota(jnp.int32, (PANEL, ROWS), 0) + offset[p]
+            onehot[p] = jnp.where(here == want, 1.0, 0.0).astype(BF16)
+
+    st = {}
 
     def wait(name):
         for cp in st[name]:
@@ -175,7 +181,7 @@
             st["fx", u].append(send(part, part, gx_s.at[u, 2 + i], gx_r.at[u, 2 + i], at_x(to)))
 
     mine = block_of(wb, WB)
-    across = block_of(core * 8 + (half_band + 4) % 8, WB)
+    pair = block_of(wb // 2, 2 * WB)
     own_lanes, panel_lanes = pl.ds(0, ROWS), pl.ds(ROWS, NPANEL * PANEL)
 
     def band_sum(_):
@@ -186,7 +192,7 @@
         total[:, Q : Q + ROWS] = acc
         st["e"] = [
             send(total.at[:, pl.ds(ROWS, Q)], total.at[:, pl.ds(0, Q)], e_s.at[0], e_r.at[0], at_c(1)),
-            send(total.at[:, pl.ds(Q, Q)], total.at[:, pl.ds(ROWS + Q, Q)], e_s.at[1], e_r.at[1], at_c(NCHAN - 1)),
+            send(total.at[:, pl.ds(Q, Q)], total.at[:, pl.ds(ROWS + Q, Q)], e_s.at[1], e_r.at[1], at_c(15)),
         ]
 
     def window(_):
@@ -236,10 +242,8 @@
         st[there] = []
         for d in range(1, 4):
             t = (c, b // 8 * 8 + (b % 8 + 2 * d) % 8)
-            for i, rows in enumerate((mine, across)):
-                part = means.at[rows, lanes]
-                s = sem + 2 * d - 1 + i
-                st[there].append(send(part, part, gb_s.at[s], gb_r.at[s], t))
+            part = means.at[pair, lanes]
+            st[there].append(send(part, part, gb_s.at[sem + d], gb_r.at[sem + d], t))
 
     def to_core(here, there, lanes, sem):
         wait(here)
@@ -287,6 +291,7 @@
         stores[-1].start()
 
     steps = {
+        "raw": raw, "power": own_power, "prepare": prepare,
         "pick": pick, "share_z": share_z, "pass_z": pass_z, "share_x": share_x, "pass_x": pass_x, "multiply": multiply,
         "band_sum": band_sum, "window": window, "choose": choose, "gathered": gathered,
         "own_y": lambda _: along_y("oz", "oy", own_lanes, 0),
@@ -304,10 +309,23 @@
         cp.wait()
 
 
+def deliver_kernel(src, dst, held, in_sem, out_sem):
+    pieces = [(p, f, k) for p in range(NPANEL) for f in range(2) for k in range(2)]
+    come = [pltpu.make_async_copy(src.at[i], held.at[i], in_sem.at[n]) for n, i in enumerate(pieces)]
+    go = [pltpu.make_async_copy(held.at[i], dst.at[i], out_sem.at[n]) for n, i in enumerate(pieces)]
+    for cp in come:
+        cp.start()
+    for one, two in zip(come, go):
+        one.wait()
+        two.start()
+    for cp in go:
+        cp.wait()
+
+
 def local(spectra, half_width, panel_block, panel_offset):
     dma = pltpu.SemaphoreType.DMA
     hbm = pl.BlockSpec(memory_space=pltpu.HBM)
-    return pl.pallas_call(
+    products = pl.pallas_call(
         move_kernel,
         out_shape=jax.ShapeDtypeStruct((NPANEL, 2, 2, ROWS, PANEL), BF16),
         in_specs=[hbm] * 4,
@@ -345,6 +363,15 @@
         ),
         name="cross_spectra",
     )(spectra, half_width, panel_block, panel_offset)
+    return pl.pallas_call(
+        deliver_kernel,
+        out_shape=jax.ShapeDtypeStruct(products.shape, BF16),
+        in_specs=[hbm],
+        out_specs=hbm,
+        scratch_shapes=[pltpu.VMEM(products.shape, BF16), dma((16,)), dma((16,))],
+        compiler_params=pltpu.CompilerParams(vmem_limit_bytes=60 * 1024 * 1024),
+        name="deliver",
+    )(products)
 
 
 def solution(mesh):

time: 100 us -> 92.8 us (0.928)
  local copies, waits for them, and re-layouts: 4.57 us -> 0 us
  Pallas kernels: 95.3 us -> 92 us
    pallas_call x1, Pallas kernels: 95.3 us -> 88.2 us  [local(): pl.pallas_call(move_kernel, out_shape=jax.ShapeDtypeStruct((NPANEL, 2, 2,...]
    unnamed x1 -> x0, local copies, waits for them, and re-layouts: 4.57 us -> none
    pallas_call x0 -> x1, Pallas kernels: none -> 3.85 us  [local(): pl.pallas_call(deliver_kernel, out_shape=jax.ShapeDtypeStruct(products.sh...]
where the time goes in v3:
time: 92.8 us; the launch traced here: 92 us
  Pallas kernels  92 us (99%)
    pallas_call x1, Pallas kernels, local(): pl.pallas_call(move_kernel, out_shape=jax.ShapeDtypeStruct((NPANEL, 2, 2,...  88.2 us
    pallas_call x1, Pallas kernels, local(): pl.pallas_call(deliver_kernel, out_shape=jax.ShapeDtypeStruct(products.sh...  3.85 us

profile of v3, /device:TPU:8, one launch (start us, length us, event | category | flops | bytes accessed | tf_op | source)
XLA Modules:
  0.0 92.0 jit_solution(8471369512923276111)
XLA Ops:
  0.0 88.2 %cross_spectra.1.src = bf16[4,2,2,512,256]{4,3,2,1,0:T(8,128)(2,1)} custom-call(bf16[2,2,512,512]{3,2,1,0:T(8,128)(2,1)} %spec_hbm.1, s32[512]{0:T(512)} %width_hbm.1, s32[4]{0:T(128)} %block_hbm.1, s32[4]{0:T(128)} %offset_hbm.1), custom_call_target="tpu_custom_call" | custom-call | tf_op jit(solution)/shard_map/cross_spectra/pallas_call | solution.py:328
  88.2 3.9 %deliver.1 = bf16[4,2,2,512,256]{4,3,2,1,0:T(8,128)(2,1)} custom-call(bf16[4,2,2,512,256]{4,3,2,1,0:T(8,128)(2,1)} %cross_spectra.1.src), custom_call_target="tpu_custom_call" | custom-call | tf_op jit(solution)/shard_map/deliver/pallas_call | solution.py:366

commit v4 on v3

--- a/solution.py
+++ b/solution.py
@@ -25,15 +25,16 @@
 BF16 = jnp.bfloat16
 
 PLAN = (
-    ("raw", 0), ("power", 0), ("prepare", 0), ("pick", 1), ("raw", 3), ("band_sum", 0), ("pick", 0), ("raw", 1),
-    ("raw", 2), ("share_z", 1), ("pick", 6), ("window", 0), ("pass_z", 1), ("pick", 2), ("share_z", 0),
-    ("share_z", 6), ("share_x", 1), ("share_z", 2), ("pick", 4), ("pass_z", 6), ("pass_x", 1), ("choose", 0),
-    ("pass_z", 0), ("own_y", 0), ("share_z", 4), ("pass_z", 2), ("share_x", 6), ("gathered", 0), ("pick", 7),
-    ("share_x", 0), ("panel_y", 0), ("pass_z", 4), ("share_x", 2), ("pick", 3), ("share_z", 7),
-    ("share_x", 4), ("pick", 5), ("pass_x", 2), ("pass_x", 6), ("panel_core", 0), ("pass_x", 0), ("pass_z", 7),
-    ("own_core", 0), ("share_z", 3), ("share_z", 5), ("pass_x", 4), ("share_x", 7), ("pass_z", 3), ("panel_scale", 0),
-    ("pass_z", 5), ("share_x", 3), ("own_norm", 0), ("share_x", 5), ("own_norm", 1), ("multiply", 2), ("pass_x", 3),
-    ("pass_x", 7), ("multiply", 0), ("pass_x", 5), ("multiply", 1), ("multiply", 3),
+    ("raw", 0), ("power", 0), ("prepare", 0), ("raw", 1), ("pick", 0), ("pick", 1), ("merge", 0), ("merge", 1),
+    ("sum_y", 0), ("share_z", 0), ("pick", 2), ("share_z", 1), ("pick", 3), ("band_sum", 0), ("raw", 2),
+    ("pass_z", 0), ("merge", 2), ("pass_z", 1), ("merge", 3), ("raw", 3), ("window", 0), ("share_x", 0),
+    ("share_z", 2), ("pick", 4), ("share_z", 3), ("share_x", 1), ("pick", 5), ("own_y", 0), ("pass_z", 2),
+    ("merge", 4), ("pick", 6), ("pass_z", 3), ("choose", 0), ("own_core", 0), ("merge", 5), ("share_x", 2),
+    ("pick", 7), ("pass_x", 0), ("share_z", 4), ("merge", 6), ("own_norm", 1), ("share_x", 3), ("pass_x", 1),
+    ("gathered", 0), ("own_norm", 0), ("share_z", 5), ("merge", 7), ("pass_x", 2), ("pass_z", 4), ("share_z", 6),
+    ("panel_y", 0), ("pass_x", 3), ("pass_z", 5), ("share_z", 7), ("share_x", 4), ("pass_z", 6), ("share_x", 5),
+    ("pass_z", 7), ("panel_core", 0), ("share_x", 6), ("pass_x", 4), ("share_x", 7), ("panel_scale", 0),
+    ("multiply", 0), ("pass_x", 6), ("pass_x", 5), ("multiply", 1), ("pass_x", 7), ("multiply", 2), ("multiply", 3),
 )
 
 
@@ -42,9 +43,10 @@
 
 
 def move_kernel(
-    spec_hbm, width_hbm, block_hbm, offset_hbm, out_hbm,
-    spec, width, block, offset, a0, a1, a2, a3, b0, b1, b2, b3, b4, b5, b6, b7, gath, picked, onehot, power, bands, total,
-    cand, parts, means, scale, left, out, l_s, o_s, a_s, a_r, rz_s, rz_r, gz_s, gz_r, gx_s, gx_r, e_s, e_r, rb_s, rb_r, rc_s, rc_r, gc_s, gc_r, gb_s, gb_r,
+    spec_hbm, width_hbm, block_hbm, offset_hbm, out_hbm, left_hbm, right_hbm,
+    spec, width, block, offset, a0, a1, a2, a3, b0, b1, b2, b3, b4, b5, b6, b7,
+    m0, m1, m2, m3, m4, m5, m6, m7, gath, picked, onehot, power, bands, near, total,
+    cand, parts, means, scale, left, out, right, l_s, o_s, a_s, a_r, rz_s, rz_r, gz_s, gz_r, gx_s, gx_r, e_s, e_r, rb_s, rb_r, rc_s, rc_r, gc_s, gc_r, gb_s, gb_r,
 ):
     c, b = lax.axis_index("chan"), lax.axis_index("band")
     x, z = c // NZ, c % NZ
@@ -56,6 +58,7 @@
 
     wb = windows_of(b)
     a, zb = (a0, a1, a2, a3), (b0, b1, b2, b3, b4, b5, b6, b7)
+    mo = (m0, m1, m2, m3, m4, m5, m6, m7)
 
     def at_x(d):
         return ((x + d) % NX * NZ + z, b)
@@ -114,9 +117,10 @@
             for j in range(WIN // Q):
                 power[j * Q : (j + 1) * Q, i * Q : (i + 1) * Q] = acc[:, j * Q : (j + 1) * Q].T.astype(BF16)
         st["rb"] = []
-        for d in range(1, NBAND):
-            src = power.at[block_of(windows_of((b + d) % NBAND), WB), :]
-            st["rb"].append(send(src, bands.at[d], rb_s.at[d], rb_r.at[d], at_b(d)))
+        for d in range(1, 8):
+            t = b // 8 * 8 + (b + d) % 8
+            src = power.at[block_of(windows_of(t) // 2, 2 * WB), :]
+            st["rb"].append(send(src, bands.at[d], rb_s.at[d], rb_r.at[d], (c, t)))
 
     def prepare(_):
         for q in range(PLANES):
@@ -144,16 +148,32 @@
             slot = lax.rem(x - block[p] // NZ + NX, NX)
             picked[q, p] = jnp.dot(onehot[p], a[q][slot], preferred_element_type=F32).astype(BF16)
         zb[u][0] = picked[q, 2 * h : 2 * h + 2, block_of(z, R), :]
+        rows = block_of((z + 2) % NZ, R)
+        st["ro", u] = [
+            send(picked.at[q, 2 * h + i, rows, :], mo[u].at[i, 1], rz_s.at[u, 2 * i], rz_r.at[u, 2 * i], at_z(d))
+            for i, d in enumerate((3, 1))
+        ]
+        for i, d in enumerate((3, 1)):
+            mo[u][i, 0] = picked[q, 2 * h + i, block_of((z + d) % NZ, R), :]
+
+    def merge(u):
+        q, h = u // 2, u % 2
+        wait(("ro", u))
         st["rz", u] = []
-        for d in (1, 3, 2):
-            src = picked.at[q, pl.ds(2 * h, 2), block_of((z + d) % NZ, R), :]
-            st["rz", u].append(send(src, zb[u].at[d], rz_s.at[u, d], rz_r.at[u, d], at_z(d)))
+        for i, d in enumerate((3, 1)):
+            rows = block_of((z + d) % NZ, R)
+            theirs = jnp.where(block[2 * h + i] % NZ == (z + NZ - d) % NZ, 1, 0)
+            picked[q, 2 * h + i, rows, :] = mo[u][i, theirs]
+            src = picked.at[q, pl.ds(2 * h, 2), rows, :]
+            s = 3 - 2 * i
+            st["rz", u].append(send(src, zb[u].at[2 - i], rz_s.at[u, s], rz_r.at[u, s], at_z(d)))
 
     def share_z(u):
         q, h = u // 2, u % 2
         wait(("rz", u))
         for i in range(2):
-            slot = lax.rem(z - block[2 * h + i] % NZ + NZ, NZ)
+            away = lax.rem(z - block[2 * h + i] % NZ + NZ, NZ)
+            slot = jnp.minimum(away, 2) if i == 0 else away - away // 2
             gath[q // 2, 2 * h + i, q % 2, block_of(z, R), block_of(x, Q)] = zb[u][slot, i]
         part = gath.at[q // 2, pl.ds(2 * h, 2), q % 2, block_of(z, R), block_of(x, Q)]
         st["gz", u] = [send(part, part, gz_s.at[u, i], gz_r.at[u, i], at_z(d)) for i, d in enumerate((1, 3))]
@@ -184,12 +204,18 @@
     pair = block_of(wb // 2, 2 * WB)
     own_lanes, panel_lanes = pl.ds(0, ROWS), pl.ds(ROWS, NPANEL * PANEL)
 
+    def near_sum(_):
+        wait("rb")
+        acc = power[pair, :].astype(F32)
+        for d in range(1, 8):
+            acc = acc + bands[d].astype(F32)
+        near[0] = acc
+        other = near.at[0, block_of((wb + 1) % 2, WB), :]
+        st["rs"] = [send(other, near.at[1, pl.ds(0, WB), :], rb_s.at[8], rb_r.at[8], at_b(8))]
+
     def band_sum(_):
-        wait("rb")
-        acc = power[mine, :].astype(F32)
-        for d in range(1, NBAND):
-            acc = acc + bands[d].astype(F32)
-        total[:, Q : Q + ROWS] = acc
+        wait("rs")
+        total[:, Q : Q + ROWS] = near[0, block_of(wb % 2, WB), :] + near[1, 0:WB, :]
         st["e"] = [
             send(total.at[:, pl.ds(ROWS, Q)], total.at[:, pl.ds(0, Q)], e_s.at[0], e_r.at[0], at_c(1)),
             send(total.at[:, pl.ds(Q, Q)], total.at[:, pl.ds(ROWS + Q, Q)], e_s.at[1], e_r.at[1], at_c(15)),
@@ -250,9 +276,12 @@
         part = means.at[block_of(core, WIN // 2), lanes]
         st[there] = [send(part, part, gb_s.at[sem], gb_r.at[sem], (c, half_band * 2 + (core + 1) % 2))]
 
+    stores, owned = [], []
+
     def own_norm(half):
-        if half == 0:
+        if not owned:
             wait("ok")
+        owned.append(half)
         for i in range(2 * half, 2 * half + 2):
             for j in range(WIN // Q):
                 s = root(means[j * Q : (j + 1) * Q, i * Q : (i + 1) * Q].astype(F32)).T
@@ -260,6 +289,9 @@
                     for k in range(2):
                         v = spec[f, k, i * Q : (i + 1) * Q, j * Q : (j + 1) * Q].astype(F32)
                         left[f, i * Q : (i + 1) * Q, k * WIN + j * Q : k * WIN + (j + 1) * Q] = (v * s).astype(BF16)
+        rows = pl.ds(half * 2 * Q, 2 * Q)
+        stores.append(pltpu.make_async_copy(left.at[1, rows], left_hbm.at[rows], o_s.at[4 + half]))
+        stores[-1].start()
 
     def panel_scale(_):
         wait("pk")
@@ -271,8 +303,6 @@
                         means[j * Q : (j + 1) * Q, lanes].astype(F32)
                     ).T
 
-    stores = []
-
     def multiply(v):
         f, h = v // 2, v % 2
         wait(("fx", 4 * f + h))
@@ -286,14 +316,22 @@
                 out[p, f, k] = (gram * WIN ** (-0.5)).astype(BF16)
             return carry
 
-        lax.fori_loop(2 * h, 2 * h + 2, body, 0)
-        stores.append(pltpu.make_async_copy(out.at[pl.ds(2 * h, 2), f], out_hbm.at[pl.ds(2 * h, 2), f], o_s.at[v]))
+        if v < 3:
+            lax.fori_loop(2 * h, 2 * h + 2, body, 0)
+        else:
+            for i in range(2):
+                for k in range(2):
+                    right[i, :, k * WIN : (k + 1) * WIN] = (gath[1, 2 + i, k].astype(F32) * scale[2 + i]).astype(BF16)
+            src, dst = right, right_hbm
+        if v < 3:
+            src, dst = out.at[pl.ds(2 * h, 2), f], out_hbm.at[v]
+        stores.append(pltpu.make_async_copy(src, dst, o_s.at[v]))
         stores[-1].start()
 
     steps = {
         "raw": raw, "power": own_power, "prepare": prepare,
-        "pick": pick, "share_z": share_z, "pass_z": pass_z, "share_x": share_x, "pass_x": pass_x, "multiply": multiply,
-        "band_sum": band_sum, "window": window, "choose": choose, "gathered": gathered,
+        "pick": pick, "merge": merge, "share_z": share_z, "pass_z": pass_z, "share_x": share_x, "pass_x": pass_x, "multiply": multiply,
+        "sum_y": near_sum, "band_sum": band_sum, "window": window, "choose": choose, "gathered": gathered,
         "own_y": lambda _: along_y("oz", "oy", own_lanes, 0),
         "own_core": lambda _: to_core("oy", "ok", own_lanes, 7),
         "panel_y": lambda _: along_y("pz", "py", panel_lanes, 8),
@@ -309,27 +347,48 @@
         cp.wait()
 
 
-def deliver_kernel(src, dst, held, in_sem, out_sem):
-    pieces = [(p, f, k) for p in range(NPANEL) for f in range(2) for k in range(2)]
-    come = [pltpu.make_async_copy(src.at[i], held.at[i], in_sem.at[n]) for n, i in enumerate(pieces)]
-    go = [pltpu.make_async_copy(held.at[i], dst.at[i], out_sem.at[n]) for n, i in enumerate(pieces)]
-    for cp in come:
+def finish_kernel(products, left_hbm, right_hbm, out, held, left, right, fresh, in_sem, out_sem):
+    first = [
+        pltpu.make_async_copy(left_hbm, left, in_sem.at[0]),
+        pltpu.make_async_copy(right_hbm.at[0], right.at[0], in_sem.at[1]),
+        pltpu.make_async_copy(right_hbm.at[1], right.at[1], in_sem.at[2]),
+    ]
+    pieces = [(v, i) for v in range(3) for i in range(2)]
+    get = [pltpu.make_async_copy(products.at[v, i], held.at[v, i], in_sem.at[3 + n]) for n, (v, i) in enumerate(pieces)]
+    put = [
+        pltpu.make_async_copy(held.at[v, i], out.at[2 * (v % 2) + i, v // 2], out_sem.at[n])
+        for n, (v, i) in enumerate(pieces)
+    ]
+    late = [pltpu.make_async_copy(fresh.at[i], out.at[2 + i, 1], out_sem.at[6 + i]) for i in range(2)]
+    for cp in first + get:
         cp.start()
-    for one, two in zip(come, go):
-        one.wait()
-        two.start()
-    for cp in go:
+    first[0].wait()
+    for i in range(2):
+        first[1 + i].wait()
+        re, im = right[i, :, :WIN], right[i, :, WIN:]
+        for k, factor in enumerate((right[i], jnp.concatenate([-im, re], axis=1))):
+            gram = lax.dot_general(left[...], factor, (((1,), (1,)), ((), ())), preferred_element_type=F32)
+            fresh[i, k] = (gram * WIN ** (-0.5)).astype(BF16)
+        late[i].start()
+        for n in range(3 * i, 3 * i + 3):
+            get[n].wait()
+            put[n].start()
+    for cp in put + late:
         cp.wait()
 
 
 def local(spectra, half_width, panel_block, panel_offset):
     dma = pltpu.SemaphoreType.DMA
     hbm = pl.BlockSpec(memory_space=pltpu.HBM)
-    products = pl.pallas_call(
+    products, left, right = pl.pallas_call(
         move_kernel,
-        out_shape=jax.ShapeDtypeStruct((NPANEL, 2, 2, ROWS, PANEL), BF16),
+        out_shape=(
+            jax.ShapeDtypeStruct((3, 2, 2, ROWS, PANEL), BF16),
+            jax.ShapeDtypeStruct((ROWS, 2 * WIN), BF16),
+            jax.ShapeDtypeStruct((2, PANEL, 2 * WIN), BF16),
+        ),
         in_specs=[hbm] * 4,
-        out_specs=hbm,
+        out_specs=(hbm, hbm, hbm),
         scratch_shapes=[
             pltpu.VMEM((2, 2, ROWS, WIN), BF16),
             pltpu.SMEM((WIN,), jnp.int32),
@@ -337,13 +396,15 @@
             pltpu.SMEM((NPANEL,), jnp.int32),
         ]
         + [pltpu.VMEM((NX, ROWS, Q), BF16)] * 4
-        + [pltpu.VMEM((NZ, 2, R, Q), BF16)] * 8
+        + [pltpu.VMEM((3, 2, R, Q), BF16)] * 8
+        + [pltpu.VMEM((2, 2, R, Q), BF16)] * 8
         + [
             pltpu.VMEM((2, NPANEL, 2, PANEL, WIN), BF16),
             pltpu.VMEM((PLANES, NPANEL, PANEL, Q), BF16),
             pltpu.VMEM((NPANEL, PANEL, ROWS), BF16),
             pltpu.VMEM((WIN, ROWS), BF16),
-            pltpu.VMEM((NBAND, WB, ROWS), BF16),
+            pltpu.VMEM((8, 2 * WB, ROWS), BF16),
+            pltpu.VMEM((2, 2 * WB, ROWS), F32),
             pltpu.VMEM((WB, ROWS + 2 * Q), F32),
             pltpu.VMEM((WB, NPANEL * PANEL), BF16),
             pltpu.VMEM((NCHAN, 16, Q), BF16),
@@ -351,8 +412,9 @@
             pltpu.VMEM((NPANEL, PANEL, WIN), F32),
             pltpu.VMEM((2, ROWS, 2 * WIN), BF16),
             pltpu.VMEM((NPANEL, 2, 2, ROWS, PANEL), BF16),
+            pltpu.VMEM((2, PANEL, 2 * WIN), BF16),
             dma((4,)),
-            dma((4,)),
+            dma((6,)),
         ]
         + [dma((4, 4))] * 2
         + [dma((8, 4))] * 6
@@ -364,14 +426,21 @@
         name="cross_spectra",
     )(spectra, half_width, panel_block, panel_offset)
     return pl.pallas_call(
-        deliver_kernel,
-        out_shape=jax.ShapeDtypeStruct(products.shape, BF16),
-        in_specs=[hbm],
+        finish_kernel,
+        out_shape=jax.ShapeDtypeStruct((NPANEL, 2, 2, ROWS, PANEL), BF16),
+        in_specs=[hbm] * 3,
         out_specs=hbm,
-        scratch_shapes=[pltpu.VMEM(products.shape, BF16), dma((16,)), dma((16,))],
+        scratch_shapes=[
+            pltpu.VMEM((3, 2, 2, ROWS, PANEL), BF16),
+            pltpu.VMEM((ROWS, 2 * WIN), BF16),
+            pltpu.VMEM((2, PANEL, 2 * WIN), BF16),
+            pltpu.VMEM((2, 2, ROWS, PANEL), BF16),
+            dma((9,)),
+            dma((8,)),
+        ],
         compiler_params=pltpu.CompilerParams(vmem_limit_bytes=60 * 1024 * 1024),
-        name="deliver",
-    )(products)
+        name="finish",
+    )(products, left, right)
 
 
 def solution(mesh):

time: 92.8 us -> 88.8 us (0.957)
  Pallas kernels: 92 us -> 88.5 us
    pallas_call x2, Pallas kernels: 92 us -> 88.5 us  [the longest x1 84.2 us: local(): pl.pallas_call(move_kernel, out_shape=(jax.ShapeDtypeStruct((3, 2, 2, ROW...]
where the time goes in v4:
time: 88.8 us; the launch traced here: 88.7 us
  Pallas kernels  88.5 us (100%)
    pallas_call x1, Pallas kernels, local(): pl.pallas_call(move_kernel, out_shape=(jax.ShapeDtypeStruct((3, 2, 2, ROW...  84.2 us
    pallas_call x1, Pallas kernels, local(): pl.pallas_call(finish_kernel, out_shape=jax.ShapeDtypeStruct((NPANEL, 2,...  4.33 us

profile of v4, /device:TPU:8, one launch (start us, length us, event | category | flops | bytes accessed | tf_op | source)
XLA Modules:
  0.0 88.7 jit_solution(7318957029694209695)
XLA Ops:
  0.0 84.2 %cross_spectra.1 = (bf16[3,2,2,512,256]{4,3,2,1,0:T(8,128)(2,1)}, bf16[512,1024]{1,0:T(8,128)(2,1)}, bf16[2,256,1024]{2,1,0:T(8,128)(2,1)}) custom-call(bf16[2,2,512,512]{3,2,1,0:T(8,128)(2,1)} %spec_hbm.1, s32[512]{0:T(512)} %width_hbm.1, s32[4]{0:T(128)} %block_hbm.1, s32[4]{0:T(128)} %offset_hbm.1), custom_call_target="tpu_custom_call" | custom-call | tf_op jit(solution)/shard_map/cross_spectra/pallas_call | solution.py:383
  84.2 4.3 %finish.1 = bf16[4,2,2,512,256]{4,3,2,1,0:T(8,128)(2,1)} custom-call(bf16[3,2,2,512,256]{4,3,2,1,0:T(8,128)(2,1)} %get-tuple-element.8.products, bf16[512,1024]{1,0:T(8,128)(2,1)} %get-tuple-element.9.left_hbm, bf16[2,256,1024]{2,1,0:T(8,128)(2,1)} %get-tuple-element.10.right_hbm), custom_call_target="tpu_custom_call" | custom-call | tf_op jit(solution)/shard_map/finish/pallas_call | solution.py:428

commit v5 on v4

--- a/solution.py
+++ b/solution.py
@@ -26,15 +26,15 @@
 
 PLAN = (
     ("raw", 0), ("power", 0), ("prepare", 0), ("raw", 1), ("pick", 0), ("pick", 1), ("merge", 0), ("merge", 1),
-    ("sum_y", 0), ("share_z", 0), ("pick", 2), ("share_z", 1), ("pick", 3), ("band_sum", 0), ("raw", 2),
-    ("pass_z", 0), ("merge", 2), ("pass_z", 1), ("merge", 3), ("raw", 3), ("window", 0), ("share_x", 0),
-    ("share_z", 2), ("pick", 4), ("share_z", 3), ("share_x", 1), ("pick", 5), ("own_y", 0), ("pass_z", 2),
-    ("merge", 4), ("pick", 6), ("pass_z", 3), ("choose", 0), ("own_core", 0), ("merge", 5), ("share_x", 2),
-    ("pick", 7), ("pass_x", 0), ("share_z", 4), ("merge", 6), ("own_norm", 1), ("share_x", 3), ("pass_x", 1),
-    ("gathered", 0), ("own_norm", 0), ("share_z", 5), ("merge", 7), ("pass_x", 2), ("pass_z", 4), ("share_z", 6),
-    ("panel_y", 0), ("pass_x", 3), ("pass_z", 5), ("share_z", 7), ("share_x", 4), ("pass_z", 6), ("share_x", 5),
-    ("pass_z", 7), ("panel_core", 0), ("share_x", 6), ("pass_x", 4), ("share_x", 7), ("panel_scale", 0),
-    ("multiply", 0), ("pass_x", 6), ("pass_x", 5), ("multiply", 1), ("pass_x", 7), ("multiply", 2), ("multiply", 3),
+    ("sum_y", 0), ("share_z", 0), ("pick", 3), ("pick", 2), ("share_z", 1), ("band_sum", 0), ("raw", 3),
+    ("pass_z", 0), ("merge", 3), ("merge", 2), ("raw", 2), ("pass_z", 1), ("window", 0), ("share_x", 0),
+    ("share_z", 3), ("pick", 6), ("share_x", 1), ("share_z", 2), ("pick", 7), ("own_y", 0), ("pass_z", 3),
+    ("merge", 6), ("pick", 4), ("choose", 0), ("own_core", 0), ("pass_z", 2), ("merge", 7), ("share_x", 3),
+    ("pick", 5), ("share_z", 6), ("pass_x", 0), ("merge", 4), ("own_norm", 1), ("pass_x", 1), ("share_x", 2),
+    ("gathered", 0), ("own_norm", 0), ("share_z", 7), ("merge", 5), ("pass_x", 3), ("pass_z", 6), ("share_z", 4),
+    ("panel_y", 0), ("pass_z", 7), ("pass_x", 2), ("share_z", 5), ("share_x", 6), ("pass_z", 4), ("share_x", 7),
+    ("pass_z", 5), ("panel_core", 0), ("share_x", 4), ("pass_x", 6), ("share_x", 5), ("panel_scale", 0),
+    ("multiply", 1), ("pass_x", 4), ("pass_x", 7), ("multiply", 0), ("pass_x", 5), ("multiply", 2), ("multiply", 3),
 )
 
 

time: 88.8 us -> 89.4 us (level)
  no operation moved by 1% of the time
where the time goes in v5:
time: 89.4 us; the launch traced here: 88.6 us
  Pallas kernels  88.4 us (99%)
    pallas_call x1, Pallas kernels, local(): pl.pallas_call(move_kernel, out_shape=(jax.ShapeDtypeStruct((3, 2, 2, ROW...  84.1 us
    pallas_call x1, Pallas kernels, local(): pl.pallas_call(finish_kernel, out_shape=jax.ShapeDtypeStruct((NPANEL, 2,...  4.33 us

profile of v5, /device:TPU:8, one launch (start us, length us, event | category | flops | bytes accessed | tf_op | source)
XLA Modules:
  0.0 88.6 jit_solution(17933776975014861222)
XLA Ops:
  0.0 84.1 %cross_spectra.1 = (bf16[3,2,2,512,256]{4,3,2,1,0:T(8,128)(2,1)}, bf16[512,1024]{1,0:T(8,128)(2,1)}, bf16[2,256,1024]{2,1,0:T(8,128)(2,1)}) custom-call(bf16[2,2,512,512]{3,2,1,0:T(8,128)(2,1)} %spec_hbm.1, s32[512]{0:T(512)} %width_hbm.1, s32[4]{0:T(128)} %block_hbm.1, s32[4]{0:T(128)} %offset_hbm.1), custom_call_target="tpu_custom_call" | custom-call | tf_op jit(solution)/shard_map/cross_spectra/pallas_call | solution.py:383
  84.1 4.3 %finish.1 = bf16[4,2,2,512,256]{4,3,2,1,0:T(8,128)(2,1)} custom-call(bf16[3,2,2,512,256]{4,3,2,1,0:T(8,128)(2,1)} %get-tuple-element.8.products, bf16[512,1024]{1,0:T(8,128)(2,1)} %get-tuple-element.9.left_hbm, bf16[2,256,1024]{2,1,0:T(8,128)(2,1)} %get-tuple-element.10.right_hbm), custom_call_target="tpu_custom_call" | custom-call | tf_op jit(solution)/shard_map/finish/pallas_call | solution.py:428
